TPU v7x, 512 devices: a whole 4x4x16 slice. The times are simulated.
512 devices in a mesh: head: 8 (over x, core), tok: 64 (over z, y).
Axes of the slice: x: 4, y: 4, z: 16, core: 2. Of those that a mesh axis runs over, the one named last changes fastest.
Arguments:
- query_one: bfloat16 [16384, 4096], P(('head', 'tok')), may hold values from -6 to 6
- key_one: bfloat16 [16384, 4096], P(('head', 'tok')), may hold values from -6 to 6
- value_one: bfloat16 [16384, 4096], P(('head', 'tok')), may hold values from -6 to 6
- rate_one: bfloat16 [16384, 8], P(('head', 'tok')), may hold values from 0.099609375 to 1
- query_two: bfloat16 [16384, 4096], P(('head', 'tok')), may hold values from -6 to 6
- w_gate: float32 [8, 512, 512], P('head', 'tok'), may hold values from -0.25 to 0.25
- w_up: float32 [8, 512, 512], P('head', 'tok'), may hold values from -0.25 to 0.25
- w_down: float32 [8, 512, 512], P('head', 'tok'), may hold values from -0.25 to 0.25
- step_size: float32 [8], P('head'), may hold values from 0.02 to 0.08
Outputs:
- out_one: bfloat16 [16384, 4096], P(('head', 'tok'))
- out_two: bfloat16 [16384, 4096], P(('head', 'tok'))
- gate_new: float32 [8, 512, 512], P('head', 'tok')
- up_new: float32 [8, 512, 512], P('head', 'tok')
- down_new: float32 [8, 512, 512], P('head', 'tok')
All inputs are finite; a program needn't handle non-finite values.
Results may differ from a plain program's by a relative error of at most 0.011.
Values may be sent and summed in bfloat16 or wider, within the bound.
A program may use at most 64 MiB of HBM per device.

v0:
```python
import jax
import jax.numpy as jnp
from jax import lax
from jax.sharding import PartitionSpec as P


def apply_piece(query, gate_b, up_b, down_b):
    pre_gate = jnp.einsum("thd,hjd->htj", query, gate_b, preferred_element_type=jnp.float32)
    pre_up = jnp.einsum("thd,hjd->htj", query, up_b, preferred_element_type=jnp.float32)
    hidden = (pre_gate * jax.nn.sigmoid(pre_gate) * pre_up).astype(jnp.bfloat16)
    return jnp.einsum("htj,hjd->thd", hidden, down_b, preferred_element_type=jnp.float32)


def forward_piece(query, keys, targets, gate_b, up_b, down_b):
    out_term = apply_piece(query, gate_b, up_b, down_b)
    key_gate = jnp.einsum("thd,hjd->htj", keys, gate_b, preferred_element_type=jnp.float32)
    key_up = jnp.einsum("thd,hjd->htj", keys, up_b, preferred_element_type=jnp.float32)
    sigmoid_k = jax.nn.sigmoid(key_gate)
    act_k = key_gate * sigmoid_k
    hidden_k = (act_k * key_up).astype(jnp.bfloat16)
    back = jnp.einsum("thd,hjd->htj", targets, down_b, preferred_element_type=jnp.float32)
    grad_gate_pre = (back * key_up * sigmoid_k * (1.0 + key_gate * (1.0 - sigmoid_k))).astype(
        jnp.bfloat16
    )
    grad_up_pre = (back * act_k).astype(jnp.bfloat16)
    return (out_term, grad_gate_pre, grad_up_pre, hidden_k)


def gradient_rows(gate_all, up_all, hidden_all, keys, targets):
    grad_gate = jnp.einsum("htj,thd->jhd", gate_all, keys, preferred_element_type=jnp.float32)
    grad_up = jnp.einsum("htj,thd->jhd", up_all, keys, preferred_element_type=jnp.float32)
    grad_down = jnp.einsum("htj,thd->jhd", hidden_all, targets, preferred_element_type=jnp.float32)
    return jnp.stack([grad_gate, grad_up, grad_down], axis=2)


def renew(weights, grad_rows, step_size):
    grads = jnp.moveaxis(grad_rows, 0, 1)
    scale = jnp.sqrt(jnp.mean(grads * grads, axis=2, keepdims=True) + 1e-06)
    return weights - step_size[:, None, None] * grads / scale


def local(query_one, key_one, value_one, rate_one, query_two, w_gate, w_up, w_down, step_size):
    heads_local = w_gate.shape[0]
    width = w_gate.shape[2]
    moved = (
        lax.all_to_all(query_one, "head", split_axis=1, concat_axis=0, tiled=True),
        lax.all_to_all(key_one, "head", split_axis=1, concat_axis=0, tiled=True),
        lax.all_to_all(value_one, "head", split_axis=1, concat_axis=0, tiled=True),
        lax.all_to_all(rate_one, "head", split_axis=1, concat_axis=0, tiled=True),
        lax.all_to_all(query_two, "head", split_axis=1, concat_axis=0, tiled=True),
    )
    tokens = moved[0].shape[0]
    query_a = moved[0].reshape(tokens, heads_local, width)
    keys = moved[1].reshape(tokens, heads_local, width)
    values = moved[2].reshape(tokens, heads_local, width)
    rates = moved[3].astype(jnp.float32)
    query_b = moved[4].reshape(tokens, heads_local, width)
    targets = (-(rates[:, :, None] * values.astype(jnp.float32))).astype(jnp.bfloat16)
    pieces = (
        lax.all_gather(w_gate.astype(jnp.bfloat16), "tok", axis=1, tiled=True),
        lax.all_gather(w_up.astype(jnp.bfloat16), "tok", axis=1, tiled=True),
        lax.all_gather(w_down.astype(jnp.bfloat16), "tok", axis=1, tiled=True),
    )
    out_term, grad_gate_pre, grad_up_pre, hidden_k = forward_piece(
        query_a, keys, targets, pieces[0], pieces[1], pieces[2]
    )
    first_block = out_term.reshape(tokens, heads_local * width).astype(jnp.bfloat16)
    grad_local = lax.psum_scatter(
        gradient_rows(grad_gate_pre, grad_up_pre, hidden_k, keys, targets),
        "tok",
        scatter_dimension=0,
        tiled=True,
    )
    gate_new = renew(w_gate, grad_local[:, :, 0, :], step_size)
    up_new = renew(w_up, grad_local[:, :, 1, :], step_size)
    down_new = renew(w_down, grad_local[:, :, 2, :], step_size)
    pieces = (
        lax.all_gather(gate_new.astype(jnp.bfloat16), "tok", axis=1, tiled=True),
        lax.all_gather(up_new.astype(jnp.bfloat16), "tok", axis=1, tiled=True),
        lax.all_gather(down_new.astype(jnp.bfloat16), "tok", axis=1, tiled=True),
    )
    second_total = apply_piece(query_b, pieces[0], pieces[1], pieces[2])
    second_block = second_total.reshape(tokens, heads_local * width).astype(jnp.bfloat16)
    first_back, second_back = (
        lax.all_to_all(first_block, "head", split_axis=0, concat_axis=1, tiled=True),
        lax.all_to_all(second_block, "head", split_axis=0, concat_axis=1, tiled=True),
    )
    return (first_back, second_back, gate_new, up_new, down_new)


def solution(mesh):
    in_specs = (
        P(("head", "tok"), None),
        P(("head", "tok"), None),
        P(("head", "tok"), None),
        P(("head", "tok"), None),
        P(("head", "tok"), None),
        P("head", "tok", None),
        P("head", "tok", None),
        P("head", "tok", None),
        P("head"),
    )
    out_specs = (
        P(("head", "tok"), None),
        P(("head", "tok"), None),
        P("head", "tok", None),
        P("head", "tok", None),
        P("head", "tok", None),
    )
    return jax.shard_map(local, mesh=mesh, in_specs=in_specs, out_specs=out_specs, check_vma=False)
```

profile of v0, /device:TPU:1, one launch (start us, length us, event | category | flops | bytes accessed | tf_op | source)
XLA Modules:
  0.0 1364.1 jit_solution(18135310961557693874)
XLA Ops:
  7.2 1.3 copy.43
  8.4 10.1 all-to-all-start.2
  18.5 0.7 convert_element_type.143
  19.3 76.5 %all_gather.20 = bf16[1,512,512]{2,1,0:T(8,128)(2,1)S(1)} all-gather(bf16[1,8,512]{2,1,0:T(8,128)(2,1)S(1)} %convert_element_type.143), channel_id=1, replica_groups=mesh['head'=8,'tok'=64] {'tok'}, dimensions={1}, use_global_device_ids=true | all-gather | bytes 532480 | tf_op jit(solution)/shard_map/all_gather | solution.py:62
  95.8 0.7 convert_element_type.141
  96.5 73.1 %all_gather.19 = bf16[1,512,512]{2,1,0:T(8,128)(2,1)S(1)} all-gather(bf16[1,8,512]{2,1,0:T(8,128)(2,1)S(1)} %convert_element_type.141), channel_id=1, replica_groups=mesh['head'=8,'tok'=64] {'tok'}, dimensions={1}, use_global_device_ids=true | all-gather | bytes 532480 | tf_op jit(solution)/shard_map/all_gather | solution.py:61
  169.7 0.7 convert_element_type.140
  170.4 1.7 copy.66
  172.0 1.7 copy.65
  173.7 0.0 all-to-all-done.2
  173.7 55.9 %all-to-all-start.4 = ((bf16[32,8,512]{2,0,1:T(8,128)(2,1)}), bf16[32,8,512]{2,0,1:T(8,128)(2,1)S(1)}, u32[]{:S(2)}, u32[]{:S(2)}) async-start(bf16[32,8,512]{2,0,1:T(8,128)(2,1)} %bitcast.139), calls=%async_computation.4 | async-start | bytes 524288 | tf_op jit(solution)/shard_map/all_to_all | solution.py:47
  229.7 71.9 %all_gather.18 = bf16[1,512,512]{2,1,0:T(8,128)(2,1)S(1)} all-gather(bf16[1,8,512]{2,1,0:T(8,128)(2,1)S(1)} %convert_element_type.140), channel_id=1, replica_groups=mesh['head'=8,'tok'=64] {'tok'}, dimensions={1}, use_global_device_ids=true | all-gather | bytes 532480 | tf_op jit(solution)/shard_map/all_gather | solution.py:60
  301.6 0.1 reshape.421
  301.7 0.0 all-to-all-done.4
  301.7 30.4 %all-to-all-start.3 = ((bf16[32,8,512]{2,0,1:T(8,128)(2,1)}), bf16[32,8,512]{2,0,1:T(8,128)(2,1)S(1)}, u32[]{:S(2)}, u32[]{:S(2)}) async-start(bf16[32,8,512]{2,0,1:T(8,128)(2,1)} %bitcast.140), calls=%async_computation.3 | async-start | bytes 524288 | tf_op jit(solution)/shard_map/all_to_all | solution.py:48
  332.0 0.0 reduce-scatter.2.cloned.1.call-start
  332.0 0.3 fusion.12
  332.4 0.3 fusion.16
  332.7 5.8 all-to-all-done.3
  338.6 0.3 fusion.9
  338.9 0.4 convolution_bitcast_fusion.1
  339.3 0.4 convolution_bitcast_fusion.2
  339.8 0.1 fusion.4
  339.9 0.4 convolution_bitcast_fusion
  340.3 1.9 pad_maximum_fusion
  342.2 0.0 copy-start
  342.2 0.0 copy-start.1
  342.2 0.0 reduce-scatter.2.cloned.1.call-update
  342.2 0.9 copy-done
  343.2 0.7 copy.67
  343.9 4.4 all-to-all-start
  348.2 0.0 copy-done.1
  348.3 0.0 copy-start.2
  348.3 0.0 copy-start.3
  348.3 0.0 copy-start.4
  348.3 0.7 copy.64
  349.7 5.1 all-to-all-done
  354.8 4.4 all-to-all-start.5
  359.1 0.3 fusion.18
  359.5 1.3 convolution_convert_fusion.1
  360.7 665.9 %reduce-scatter.2.cloned.1.call-done = f32[8,1,3,512]{3,0,2,1:T(8,128)} async-done(((f32[512,1,3,512]{3,0,2,1:T(8,128)}), f32[8,1,3,512]{3,0,2,1:T(8,128)}) %reduce-scatter.2.cloned.1.call-update) | async-done | bytes 49168 | tf_op jit(solution)/shard_map/reduce_scatter | solution.py:68
  1026.6 0.9 multiply_reduce_fusion.1
  1027.5 0.0 copy-done.2
  1027.5 0.0 copy-done.3
  1027.6 0.0 copy-done.4
  1027.6 1.5 fusion.47
  1029.0 72.6 %all_gather.23 = bf16[1,512,512]{2,1,0:T(8,128)(2,1)S(1)} all-gather(bf16[1,8,512]{2,1,0:T(8,128)(2,1)S(1)} %get-tuple-element.14), channel_id=1, replica_groups=mesh['head'=8,'tok'=64] {'tok'}, dimensions={1}, use_global_device_ids=true | all-gather | bytes 532480 | tf_op jit(solution)/shard_map/all_gather | solution.py:79
  1101.6 73.4 %all_gather.21 = bf16[1,512,512]{2,1,0:T(8,128)(2,1)S(1)} all-gather(bf16[1,8,512]{2,1,0:T(8,128)(2,1)S(1)} %get-tuple-element.16), channel_id=1, replica_groups=mesh['head'=8,'tok'=64] {'tok'}, dimensions={1}, use_global_device_ids=true | all-gather | bytes 532480 | tf_op jit(solution)/shard_map/all_gather | solution.py:80
  1175.0 72.8 %all_gather.22 = bf16[1,512,512]{2,1,0:T(8,128)(2,1)S(1)} all-gather(bf16[1,8,512]{2,1,0:T(8,128)(2,1)S(1)} %get-tuple-element.8), channel_id=1, replica_groups=mesh['head'=8,'tok'=64] {'tok'}, dimensions={1}, use_global_device_ids=true | all-gather | bytes 532480 | tf_op jit(solution)/shard_map/all_gather | solution.py:78
  1247.8 0.0 all-to-all-done.5
  1247.8 91.3 %all-to-all-start.1 = ((bf16[8,32,512]{2,1,0:T(8,128)(2,1)}), bf16[8,32,512]{2,1,0:T(8,128)(2,1)S(1)}, u32[]{:S(2)}, u32[]{:S(2)}) async-start(bf16[8,32,512]{2,1,0:T(8,128)(2,1)} %bitcast.9), calls=%async_computation.1 | async-start | bytes 524288 | tf_op jit(solution)/shard_map/all_to_all | solution.py:85
  1339.1 0.3 convolution_bitcast_fusion.4
  1339.5 1.3 convolution_convert_fusion
  1340.7 4.9 all-to-all-done.1
  1345.6 4.4 all-to-all-start.6
  1350.0 0.7 copy.58
  1350.7 5.8 all-to-all-done.6
  1356.5 0.7 copy.59
  (4 shorter events, 0.1 us)
Async XLA Ops:
  8.4 165.3 %all-to-all-start.2 = ((bf16[32,8,1]{0,2,1:T(2,128)(2,1)}), bf16[32,8,1]{0,2,1:T(2,128)(2,1)S(1)}, u32[]{:S(2)}, u32[]{:S(2)}) async-start(bf16[32,8,1]{0,2,1:T(2,128)(2,1)} %copy.43), calls=%async_computation.2 | async-start | bytes 8192 | tf_op jit(solution)/shard_map/all_to_all | solution.py:49
  173.7 128.0 %all-to-all-start.4 = ((bf16[32,8,512]{2,0,1:T(8,128)(2,1)}), bf16[32,8,512]{2,0,1:T(8,128)(2,1)S(1)}, u32[]{:S(2)}, u32[]{:S(2)}) async-start(bf16[32,8,512]{2,0,1:T(8,128)(2,1)} %bitcast.139), calls=%async_computation.4 | async-start | bytes 524288 | tf_op jit(solution)/shard_map/all_to_all | solution.py:47
  301.7 36.9 %all-to-all-start.3 = ((bf16[32,8,512]{2,0,1:T(8,128)(2,1)}), bf16[32,8,512]{2,0,1:T(8,128)(2,1)S(1)}, u32[]{:S(2)}, u32[]{:S(2)}) async-start(bf16[32,8,512]{2,0,1:T(8,128)(2,1)} %bitcast.140), calls=%async_computation.3 | async-start | bytes 524288 | tf_op jit(solution)/shard_map/all_to_all | solution.py:48
  332.0 694.6 %reduce-scatter.2.cloned.1.call-start = ((), (), s32[]{:S(2)}) async-start(), calls=%async_computation.8 | async-start | bytes 3194880 | tf_op jit(solution)/shard_map/reduce_scatter | solution.py:68
  342.2 0.9 copy-start
  342.2 6.0 copy-start.1
  343.9 10.9 all-to-all-start
  348.3 679.3 %copy-start.2 = (f32[1,8,512]{2,1,0:T(8,128)S(1)}, f32[1,8,512]{2,1,0:T(8,128)}, u32[]{:S(2)}) copy-start(f32[1,8,512]{2,1,0:T(8,128)} %param.16) | copy-start | bytes 49156
  348.3 679.3 %copy-start.3 = (f32[1,8,512]{2,1,0:T(8,128)S(1)}, f32[1,8,512]{2,1,0:T(8,128)}, u32[]{:S(2)}) copy-start(f32[1,8,512]{2,1,0:T(8,128)} %param.15) | copy-start | bytes 49156
  348.3 679.3 %copy-start.4 = (f32[1,8,512]{2,1,0:T(8,128)S(1)}, f32[1,8,512]{2,1,0:T(8,128)}, u32[]{:S(2)}) copy-start(f32[1,8,512]{2,1,0:T(8,128)} %param.14) | copy-start | bytes 49156
  354.8 893.0 %all-to-all-start.5 = ((bf16[32,8,512]{2,0,1:T(8,128)(2,1)}), bf16[32,8,512]{2,0,1:T(8,128)(2,1)S(1)}, u32[]{:S(2)}, u32[]{:S(2)}) async-start(bf16[32,8,512]{2,0,1:T(8,128)(2,1)} %bitcast.138), calls=%async_computation.6 | async-start | bytes 524288 | tf_op jit(solution)/shard_map/all_to_all | solution.py:50
  1247.8 97.8 %all-to-all-start.1 = ((bf16[8,32,512]{2,1,0:T(8,128)(2,1)}), bf16[8,32,512]{2,1,0:T(8,128)(2,1)S(1)}, u32[]{:S(2)}, u32[]{:S(2)}) async-start(bf16[8,32,512]{2,1,0:T(8,128)(2,1)} %bitcast.9), calls=%async_computation.1 | async-start | bytes 524288 | tf_op jit(solution)/shard_map/all_to_all | solution.py:85
  1345.6 10.9 all-to-all-start.6
Sparse Core Ops, SparseCore 0:
  342.4 684.1 reduce-scatter.1
where the time goes:
time: 1370 us; the launch traced here: 1360 us
  waiting for transfers between devices  688 us (50%)
  blocking collectives  440 us (32%)
  starting transfers between devices  201 us (15%)
  between operations  14.8 us (1%)
    reduce_scatter x1, waiting for transfers between devices, local(): lax.psum_scatter(gradient_rows(grad_gate_pre, grad_up_pre, hidden_k, keys...  666 us
    all_to_all x1, starting transfers between devices, local(): lax.all_to_all(first_block, 'head', split_axis=0, concat_axis=1, tiled=True)  91.3 us
    all_gather x1, blocking collectives, local(): lax.all_gather(w_down.astype(jnp.bfloat16), 'tok', axis=1, tiled=True)  76.5 us
    all_gather x1, blocking collectives, local(): lax.all_gather(down_new.astype(jnp.bfloat16), 'tok', axis=1, tiled=True)  73.4 us
    all_gather x1, blocking collectives, local(): lax.all_gather(w_up.astype(jnp.bfloat16), 'tok', axis=1, tiled=True)  73.1 us
    all_gather x1, blocking collectives, local(): lax.all_gather(gate_new.astype(jnp.bfloat16), 'tok', axis=1, tiled=True)  72.8 us
    all_gather x1, blocking collectives, local(): lax.all_gather(up_new.astype(jnp.bfloat16), 'tok', axis=1, tiled=True)  72.6 us
    all_gather x1, blocking collectives, local(): lax.all_gather(w_gate.astype(jnp.bfloat16), 'tok', axis=1, tiled=True)  71.9 us
  transfers between devices with their start and end apart: 8, of which 5 were waited for; matrix products, arithmetic and copies ran while one was open for 1% of the time, Pallas kernels for 0%

commit v1 on v0

--- a/solution.py
+++ b/solution.py
@@ -77,7 +77,12 @@
     pieces = (
         lax.all_gather(gate_new.astype(jnp.bfloat16), "tok", axis=1, tiled=True),
         lax.all_gather(up_new.astype(jnp.bfloat16), "tok", axis=1, tiled=True),
-        lax.all_gather(down_new.astype(jnp.bfloat16), "tok", axis=1, tiled=True),
+        jnp.concatenate(
+            lax.all_to_all(
+                jnp.stack([down_new.astype(jnp.bfloat16)] * lax.axis_size("tok")), "tok", 0, 0
+            ),
+            axis=1,
+        ),
     )
     second_total = apply_piece(query_b, pieces[0], pieces[1], pieces[2])
     second_block = second_total.reshape(tokens, heads_local * width).astype(jnp.bfloat16)

time: 1370 us -> 1310 us (0.956)
  blocking collectives: 440 us -> 387 us
  starting transfers between devices: 201 us -> 187 us
    all_gather x1 -> x0, blocking collectives: 73.4 us -> none  [local(): lax.all_gather(down_new.astype(jnp.bfloat16), 'tok', axis=1, tiled=True)]
    all_to_all x1, starting transfers between devices: 91.3 us -> 54.1 us  [local(): lax.all_to_all(first_block, 'head', split_axis=0, concat_axis=1, tiled=True)]
    all_gather x1, blocking collectives: 72.6 us -> 91.7 us  [local(): lax.all_gather(up_new.astype(jnp.bfloat16), 'tok', axis=1, tiled=True)]
  transfers between devices with their start and end apart: 8 -> 9, of which waited for: 5 -> 5; matrix products, arithmetic and copies ran while one was open for 1% -> 1% of each run, Pallas kernels for 0% -> 0%
where the time goes in v1:
time: 1310 us
  waiting for transfers between devices  699 us (53%)
  blocking collectives  387 us (30%)
  starting transfers between devices  187 us (14%)
  between operations  14.8 us (1%)
    reduce_scatter x1, waiting for transfers between devices, local(): lax.psum_scatter(gradient_rows(grad_gate_pre, grad_up_pre, hidden_k, keys...  677 us
    all_gather x1, blocking collectives, local(): lax.all_gather(up_new.astype(jnp.bfloat16), 'tok', axis=1, tiled=True)  91.7 us
    all_gather x1, blocking collectives, local(): lax.all_gather(w_down.astype(jnp.bfloat16), 'tok', axis=1, tiled=True)  76.5 us
    all_gather x1, blocking collectives, local(): lax.all_gather(gate_new.astype(jnp.bfloat16), 'tok', axis=1, tiled=True)  73.2 us
    all_gather x1, blocking collectives, local(): lax.all_gather(w_up.astype(jnp.bfloat16), 'tok', axis=1, tiled=True)  73.1 us
    all_gather x1, blocking collectives, local(): lax.all_gather(w_gate.astype(jnp.bfloat16), 'tok', axis=1, tiled=True)  71.9 us
    all_to_all x1, starting transfers between devices, local(): lax.all_to_all(key_one, 'head', split_axis=1, concat_axis=0, tiled=True)  55.9 us
    all_to_all x1, starting transfers between devices, local(): lax.all_to_all(first_block, 'head', split_axis=0, concat_axis=1, tiled=True)  54.1 us
  transfers between devices with their start and end apart: 9, of which 5 were waited for; matrix products, arithmetic and copies ran while one was open for 1% of the time, Pallas kernels for 0%

profile of v1, /device:TPU:1, one launch (start us, length us, event | category | flops | bytes accessed | tf_op | source)
XLA Modules:
  0.0 1308.5 jit_solution(12223803940045427696)
XLA Ops:
  7.2 1.3 copy.43
  8.4 10.1 all-to-all-start.2
  18.5 0.7 convert_element_type.145
  19.3 76.5 %all_gather.17 = bf16[1,512,512]{2,1,0:T(8,128)(2,1)S(1)} all-gather(bf16[1,8,512]{2,1,0:T(8,128)(2,1)S(1)} %convert_element_type.145), channel_id=1, replica_groups=mesh['head'=8,'tok'=64] {'tok'}, dimensions={1}, use_global_device_ids=true | all-gather | bytes 532480 | tf_op jit(solution)/shard_map/all_gather | solution.py:62
  95.8 0.7 convert_element_type.143
  96.5 73.1 %all_gather.16 = bf16[1,512,512]{2,1,0:T(8,128)(2,1)S(1)} all-gather(bf16[1,8,512]{2,1,0:T(8,128)(2,1)S(1)} %convert_element_type.143), channel_id=1, replica_groups=mesh['head'=8,'tok'=64] {'tok'}, dimensions={1}, use_global_device_ids=true | all-gather | bytes 532480 | tf_op jit(solution)/shard_map/all_gather | solution.py:61
  169.7 0.7 convert_element_type.142
  170.4 1.7 copy.66
  172.0 1.7 copy.65
  173.7 0.0 all-to-all-done.2
  173.7 55.9 %all-to-all-start.4 = ((bf16[32,8,512]{2,0,1:T(8,128)(2,1)}), bf16[32,8,512]{2,0,1:T(8,128)(2,1)S(1)}, u32[]{:S(2)}, u32[]{:S(2)}) async-start(bf16[32,8,512]{2,0,1:T(8,128)(2,1)} %bitcast.141), calls=%async_computation.4 | async-start | bytes 524288 | tf_op jit(solution)/shard_map/all_to_all | solution.py:47
  229.7 71.9 %all_gather.15 = bf16[1,512,512]{2,1,0:T(8,128)(2,1)S(1)} all-gather(bf16[1,8,512]{2,1,0:T(8,128)(2,1)S(1)} %convert_element_type.142), channel_id=1, replica_groups=mesh['head'=8,'tok'=64] {'tok'}, dimensions={1}, use_global_device_ids=true | all-gather | bytes 532480 | tf_op jit(solution)/shard_map/all_gather | solution.py:60
  301.6 0.1 reshape.426
  301.7 0.0 all-to-all-done.4
  301.7 30.4 %all-to-all-start.3 = ((bf16[32,8,512]{2,0,1:T(8,128)(2,1)}), bf16[32,8,512]{2,0,1:T(8,128)(2,1)S(1)}, u32[]{:S(2)}, u32[]{:S(2)}) async-start(bf16[32,8,512]{2,0,1:T(8,128)(2,1)} %bitcast.142), calls=%async_computation.3 | async-start | bytes 524288 | tf_op jit(solution)/shard_map/all_to_all | solution.py:48
  332.0 0.0 reduce-scatter.2.cloned.1.call-start
  332.0 0.3 fusion.12
  332.4 0.3 fusion.16
  332.7 5.8 all-to-all-done.3
  338.6 0.3 fusion.9
  338.9 0.4 convolution_bitcast_fusion.1
  339.3 0.4 convolution_bitcast_fusion.2
  339.8 0.1 fusion.4
  339.9 0.4 convolution_bitcast_fusion
  340.3 1.9 pad_maximum_fusion
  342.2 0.0 copy-start
  342.2 0.0 copy-start.1
  342.2 0.0 copy-start.2
  342.2 0.0 copy-start.3
  342.2 0.0 copy-start.4
  342.2 0.0 reduce-scatter.2.cloned.1.call-update
  342.3 0.9 copy-done
  343.2 0.7 copy.67
  343.9 4.4 all-to-all-start
  348.2 0.0 copy-done.1
  348.2 0.7 copy.64
  349.6 677.2 %reduce-scatter.2.cloned.1.call-done = f32[8,1,3,512]{3,0,2,1:T(8,128)} async-done(((f32[512,1,3,512]{3,0,2,1:T(8,128)}), f32[8,1,3,512]{3,0,2,1:T(8,128)}) %reduce-scatter.2.cloned.1.call-update) | async-done | bytes 49168 | tf_op jit(solution)/shard_map/reduce_scatter | solution.py:68
  1026.8 0.9 multiply_reduce_fusion.1
  1027.8 0.0 all-to-all-done
  1027.8 16.2 %all-to-all-start.6 = ((bf16[32,8,512]{2,0,1:T(8,128)(2,1)}), bf16[32,8,512]{2,0,1:T(8,128)(2,1)S(1)}, u32[]{:S(2)}, u32[]{:S(2)}) async-start(bf16[32,8,512]{2,0,1:T(8,128)(2,1)} %bitcast.140), calls=%async_computation.7 | async-start | bytes 524288 | tf_op jit(solution)/shard_map/all_to_all | solution.py:50
  1043.9 0.0 copy-done.2
  1043.9 0.0 copy-done.3
  1043.9 0.0 copy-done.4
  1044.0 1.5 fusion.47
  1045.4 5.0 all-to-all-done.6
  1050.4 0.8 stack.14
  1051.3 11.3 all-to-all-start.5
  1062.6 0.3 fusion.18
  1062.9 1.3 convolution_convert_fusion.1
  1064.2 91.7 %all_gather.19 = bf16[1,512,512]{2,1,0:T(8,128)(2,1)S(1)} all-gather(bf16[1,8,512]{2,1,0:T(8,128)(2,1)S(1)} %get-tuple-element.14), channel_id=1, replica_groups=mesh['head'=8,'tok'=64] {'tok'}, dimensions={1}, use_global_device_ids=true | all-gather | bytes 532480 | tf_op jit(solution)/shard_map/all_gather | solution.py:79
  1155.9 73.2 %all_gather.18 = bf16[1,512,512]{2,1,0:T(8,128)(2,1)S(1)} all-gather(bf16[1,8,512]{2,1,0:T(8,128)(2,1)S(1)} %get-tuple-element.8), channel_id=1, replica_groups=mesh['head'=8,'tok'=64] {'tok'}, dimensions={1}, use_global_device_ids=true | all-gather | bytes 532480 | tf_op jit(solution)/shard_map/all_gather | solution.py:78
  1229.1 0.3 convolution_bitcast_fusion.4
  1229.5 0.0 all-to-all-done.5
  1229.5 54.1 %all-to-all-start.1 = ((bf16[8,32,512]{2,1,0:T(8,128)(2,1)}), bf16[8,32,512]{2,1,0:T(8,128)(2,1)S(1)}, u32[]{:S(2)}, u32[]{:S(2)}) async-start(bf16[8,32,512]{2,1,0:T(8,128)(2,1)} %bitcast.9), calls=%async_computation.1 | async-start | bytes 524288 | tf_op jit(solution)/shard_map/all_to_all | solution.py:90
  1283.5 1.3 convolution_convert_fusion
  1284.8 5.3 all-to-all-done.1
  1290.1 4.4 all-to-all-start.7
  1294.4 0.7 copy.58
  1295.1 5.8 all-to-all-done.7
  1300.9 0.7 copy.59
  (4 shorter events, 0.1 us)
Async XLA Ops:
  8.4 165.3 %all-to-all-start.2 = ((bf16[32,8,1]{0,2,1:T(2,128)(2,1)}), bf16[32,8,1]{0,2,1:T(2,128)(2,1)S(1)}, u32[]{:S(2)}, u32[]{:S(2)}) async-start(bf16[32,8,1]{0,2,1:T(2,128)(2,1)} %copy.43), calls=%async_computation.2 | async-start | bytes 8192 | tf_op jit(solution)/shard_map/all_to_all | solution.py:49
  173.7 128.0 %all-to-all-start.4 = ((bf16[32,8,512]{2,0,1:T(8,128)(2,1)}), bf16[32,8,512]{2,0,1:T(8,128)(2,1)S(1)}, u32[]{:S(2)}, u32[]{:S(2)}) async-start(bf16[32,8,512]{2,0,1:T(8,128)(2,1)} %bitcast.141), calls=%async_computation.4 | async-start | bytes 524288 | tf_op jit(solution)/shard_map/all_to_all | solution.py:47
  301.7 36.9 %all-to-all-start.3 = ((bf16[32,8,512]{2,0,1:T(8,128)(2,1)}), bf16[32,8,512]{2,0,1:T(8,128)(2,1)S(1)}, u32[]{:S(2)}, u32[]{:S(2)}) async-start(bf16[32,8,512]{2,0,1:T(8,128)(2,1)} %bitcast.142), calls=%async_computation.3 | async-start | bytes 524288 | tf_op jit(solution)/shard_map/all_to_all | solution.py:48
  332.0 694.8 %reduce-scatter.2.cloned.1.call-start = ((), (), s32[]{:S(2)}) async-start(), calls=%async_computation.9 | async-start | bytes 3194880 | tf_op jit(solution)/shard_map/reduce_scatter | solution.py:68
  342.2 0.9 copy-start
  342.2 6.0 copy-start.1
  342.2 701.7 %copy-start.2 = (f32[1,8,512]{2,1,0:T(8,128)S(1)}, f32[1,8,512]{2,1,0:T(8,128)}, u32[]{:S(2)}) copy-start(f32[1,8,512]{2,1,0:T(8,128)} %param.16) | copy-start | bytes 49156
  342.2 701.7 %copy-start.3 = (f32[1,8,512]{2,1,0:T(8,128)S(1)}, f32[1,8,512]{2,1,0:T(8,128)}, u32[]{:S(2)}) copy-start(f32[1,8,512]{2,1,0:T(8,128)} %param.15) | copy-start | bytes 49156
  342.2 701.7 %copy-start.4 = (f32[1,8,512]{2,1,0:T(8,128)S(1)}, f32[1,8,512]{2,1,0:T(8,128)}, u32[]{:S(2)}) copy-start(f32[1,8,512]{2,1,0:T(8,128)} %param.14) | copy-start | bytes 49156
  343.9 683.9 %all-to-all-start = ((bf16[32,8,512]{2,0,1:T(8,128)(2,1)}), bf16[32,8,512]{2,0,1:T(8,128)(2,1)S(1)}, u32[]{:S(2)}, u32[]{:S(2)}) async-start(bf16[32,8,512]{2,0,1:T(8,128)(2,1)} %bitcast.143), calls=%async_computation | async-start | bytes 524288 | tf_op jit(solution)/shard_map/all_to_all | solution.py:46
  1027.8 22.7 %all-to-all-start.6 = ((bf16[32,8,512]{2,0,1:T(8,128)(2,1)}), bf16[32,8,512]{2,0,1:T(8,128)(2,1)S(1)}, u32[]{:S(2)}, u32[]{:S(2)}) async-start(bf16[32,8,512]{2,0,1:T(8,128)(2,1)} %bitcast.140), calls=%async_computation.7 | async-start | bytes 524288 | tf_op jit(solution)/shard_map/all_to_all | solution.py:50
  1051.3 178.2 %all-to-all-start.5 = ((bf16[64,1,8,512]{3,2,1,0:T(8,128)(2,1)}), bf16[64,1,8,512]{3,2,1,0:T(8,128)(2,1)S(1)}, u32[]{:S(2)}, u32[]{:S(2)}) async-start(bf16[64,1,8,512]{3,2,1,0:T(8,128)(2,1)} %stack.14), calls=%async_computation.6 | async-start | bytes 1048576 | tf_op jit(solution)/shard_map/all_to_all | solution.py:81
  1229.5 60.6 %all-to-all-start.1 = ((bf16[8,32,512]{2,1,0:T(8,128)(2,1)}), bf16[8,32,512]{2,1,0:T(8,128)(2,1)S(1)}, u32[]{:S(2)}, u32[]{:S(2)}) async-start(bf16[8,32,512]{2,1,0:T(8,128)(2,1)} %bitcast.9), calls=%async_computation.1 | async-start | bytes 524288 | tf_op jit(solution)/shard_map/all_to_all | solution.py:90
  1290.1 10.9 all-to-all-start.7
Sparse Core Ops, SparseCore 0:
  342.4 684.4 reduce-scatter.1
